TPU v7x, 32 devices: a whole 2x2x4 slice. The times are simulated.
32 devices in a mesh: groups: 1, expert: 16 (over z, y, core), tensor: 2 (over x).
Axes of the slice: x: 2, y: 2, z: 4, core: 2. Of those that a mesh axis runs over, the one named last changes fastest.
Arguments:
- tokens: bfloat16 [2048, 4096], P(('groups', 'expert')), may hold values from -6 to 6
- expert_ids: int32 [2048, 8], P(('groups', 'expert')), may hold values from 0 to 15, all different within a row; in each aligned block of 128 rows (0 to 127, 128 to 255, ...) at most 96 rows name the same one
- route_weights: float32 [2048, 8], P(('groups', 'expert')), may hold values from 0.1 to 1
- gate_w: bfloat16 [16, 4096, 1536], P('expert', None, 'tensor'), may hold values from -0.09375 to 0.09375
- up_w: bfloat16 [16, 4096, 1536], P('expert', None, 'tensor'), may hold values from -0.09375 to 0.09375
- down_w: bfloat16 [16, 1536, 4096], P('expert', 'tensor'), may hold values from -0.15625 to 0.15625
Outputs:
- moe_out: bfloat16 [2048, 4096], P(('groups', 'expert'), 'tensor')
Inputs may be any that keep to these rules, and one draw needn't show every extreme that they name: `expert_ids`: each row names 8 different experts. Among the rows of one device (aligned blocks of 128 rows) no expert is named more than 96 times, a bound that some block reaches.
All inputs are finite; a program needn't handle non-finite values.
Results may differ from a plain program's by a relative error of at most 0.014.
Values may be sent and summed in bfloat16 or wider, within the bound.
No kernel may reach another device: no remote copies, remote signals or barrier semaphores. Data moves between devices by JAX's collectives and lax.ppermute only.
A program may use at most 128 MiB of HBM per device.

v0:
```python
import jax
import jax.numpy as jnp
from jax import lax
from jax.sharding import PartitionSpec as P


def shards(tokens, expert_ids, route_weights, gate_w, up_w, down_w):
    tok_rows, width = tokens.shape
    top_count = expert_ids.shape[1]
    local_experts = gate_w.shape[0]
    expert_devices = lax.axis_size("expert")
    experts_all = local_experts * expert_devices
    capacity = min(tok_rows, 3 * tok_rows * top_count // (2 * experts_all))
    flat_ids = expert_ids.reshape(-1)
    onehot = (flat_ids[:, None] == jnp.arange(experts_all, dtype=jnp.int32)[None, :]).astype(
        jnp.int32
    )
    before = jnp.cumsum(onehot, axis=0) - onehot
    slot = jnp.sum(before * onehot, axis=1)
    destination = flat_ids * capacity + slot
    token_index = jnp.arange(tok_rows * top_count, dtype=jnp.int32) // top_count
    source = jnp.zeros((experts_all * capacity,), jnp.int32).at[destination].set(token_index)
    filled = jnp.zeros((experts_all * capacity,), jnp.bool_).at[destination].set(True)
    outgoing = jnp.where(filled[:, None], tokens[source], jnp.zeros((), tokens.dtype))
    outgoing = outgoing.reshape(experts_all, capacity, tokens.shape[1])
    received = lax.all_to_all(outgoing, "expert", split_axis=0, concat_axis=0, tiled=True)
    slots_in = received.shape[1]
    rows = received.reshape(expert_devices, local_experts, slots_in, width)
    rows = rows.transpose(1, 0, 2, 3).reshape(local_experts, expert_devices * slots_in, width)
    gate = jnp.einsum("erd,edf->erf", rows, gate_w, preferred_element_type=jnp.float32)
    up_part = jnp.einsum("erd,edf->erf", rows, up_w, preferred_element_type=jnp.float32)
    hidden = (jax.nn.silu(gate) * up_part).astype(jnp.bfloat16)
    partial_value = jnp.einsum("erf,efd->erd", hidden, down_w, preferred_element_type=jnp.float32)
    summed = lax.psum_scatter(
        partial_value.astype(jnp.bfloat16), "tensor", scatter_dimension=2, tiled=True
    )
    share = summed.shape[2]
    going_back = summed.reshape(local_experts, expert_devices, slots_in, share)
    going_back = going_back.transpose(1, 0, 2, 3).reshape(experts_all, slots_in, share)
    returned = lax.all_to_all(going_back, "expert", split_axis=0, concat_axis=0, tiled=True)
    share_cols = returned.shape[2]
    flat_back = returned.reshape(experts_all * capacity, share_cols)
    picked = flat_back[destination].reshape(tok_rows, top_count, share_cols)
    mixed = jnp.einsum("tk,tkd->td", route_weights, picked.astype(jnp.float32))
    return mixed.astype(jnp.bfloat16)


def solution(mesh):
    in_specs = (
        P(("groups", "expert"), None),
        P(("groups", "expert"), None),
        P(("groups", "expert"), None),
        P("expert", None, "tensor"),
        P("expert", None, "tensor"),
        P("expert", "tensor", None),
    )
    out_specs = P(("groups", "expert"), "tensor")
    return jax.shard_map(shards, mesh=mesh, in_specs=in_specs, out_specs=out_specs, check_vma=False)
```

profile of v0, /device:TPU:13, one launch (start us, length us, event | category | flops | bytes accessed | tf_op | source)
XLA Modules:
  0.0 667.3 jit_solution(3514439401842417183)
XLA Ops:
  6.5 0.0 copy-start
  6.5 0.9 copy.10
  7.4 0.1 eq.29
  7.5 0.1 eq.25
  7.6 0.7 broadcast_multiply_fusion
  8.3 4.5 reduce-window.6
  12.8 0.1 slice.12
  12.9 0.1 copy.12
  13.1 0.1 copy.13
  13.1 0.1 broadcast_add_fusion
  13.2 0.1 copy.9
  13.3 0.1 mul.30
  13.5 4.3 scatter_custom_fusion.1
  17.9 4.3 scatter_custom_fusion
  22.2 0.1 broadcast_in_dim.30
  22.3 9.5 %gather_fusion = bf16[1536,4096]{1,0:T(8,128)(2,1)} fusion(bf16[128,4096]{1,0:T(8,128)(2,1)S(1)} %copy-done, s32[2048]{0:T(1024)S(1)} %pad_clamp_fusion), kind=kCustom, calls=%fused_computation | custom fusion | bytes 25171968 | tf_op jit(solution)/shard_map/gather | solution.py:24
  31.8 6.4 broadcast_select_fusion
  38.2 0.0 copy-start.3
  38.2 278.6 %all_to_all.10 = bf16[16,96,4096]{2,1,0:T(8,128)(2,1)S(1)} all-to-all(bf16[16,96,4096]{2,1,0:T(8,128)(2,1)S(1)} %broadcast_select_fusion), channel_id=1, replica_groups=mesh['groups'=1,'expert'=16,'tensor'=2] {'expert'}, dimensions={0} | all-to-all | bytes 25165824 | tf_op jit(solution)/shard_map/all_to_all | solution.py:26
  316.8 11.4 %fusion.2 = f32[1536,768]{1,0:T(8,128)} fusion(bf16[1536,4096]{1,0:T(8,128)(2,1)S(1)} %bitcast.49, bf16[1,4096,768]{2,1,0:T(8,128)(2,1)S(1)} %copy-done.3), kind=kOutput, calls=%fused_computation.8 | convolution fusion | flops 9663676416 | bytes 23592960 | tf_op jit(solution)/shard_map/erd,edf->erf/dot_general | solution.py:31
  328.3 13.5 %multiply_convert_fusion = bf16[1536,768]{1,0:T(8,128)(2,1)S(1)} fusion(f32[1536,768]{1,0:T(8,128)} %fusion.2, bf16[1536,4096]{1,0:T(8,128)(2,1)S(1)} %bitcast.50, bf16[1,4096,768]{2,1,0:T(8,128)(2,1)} %param.9), kind=kOutput, calls=%fused_computation.12 | convolution fusion | flops 9670754304 | bytes 25952256 | tf_op jit(solution)/shard_map/erd,edf->erf/dot_general | solution.py:30
  341.8 0.0 slice-done
  341.8 0.0 slice-done.1
  341.8 12.4 %fusion = bf16[1,1536,4096]{2,1,0:T(8,128)(2,1)} fusion(bf16[1536,768]{1,0:T(8,128)(2,1)S(1)} %multiply_convert_fusion, bf16[1,768,4096]{2,1,0:T(8,128)(2,1)S(1)} %bitcast.60), kind=kOutput, calls=%fused_computation.5 | convolution fusion | flops 9669967872 | bytes 21233664 | tf_op jit(solution)/shard_map/erf,efd->erd/dot_general | solution.py:33
  354.2 0.0 reduce-scatter.2.cloned.1.call-update
  354.2 145.3 %reduce-scatter.2.cloned.1.call-done = bf16[1,1536,2048]{2,1,0:T(8,128)(2,1)} async-done(((bf16[1,1536,4096]{2,1,0:T(8,128)(2,1)}), bf16[1,1536,2048]{2,1,0:T(8,128)(2,1)}) %reduce-scatter.2.cloned.1.call-update) | async-done | bytes 6291472 | tf_op jit(solution)/shard_map/reduce_scatter | solution.py:34
  499.5 6.5 all-to-all-start.1
  506.0 0.1 copy.14
  506.2 137.2 %all-to-all-done.1 = bf16[16,96,2048]{2,1,0:T(8,128)(2,1)} async-done(((bf16[16,96,2048]{2,1,0:T(8,128)(2,1)}), bf16[16,96,2048]{2,1,0:T(8,128)(2,1)}, u32[]{:S(2)}, u32[]{:S(2)}) %all-to-all-start.1) | async-done | bytes 6291488 | tf_op jit(solution)/shard_map/all_to_all | solution.py:40
  643.4 12.5 %gather_fusion.1 = bf16[1024,2048]{1,0:T(8,128)(2,1)} fusion(bf16[1536,2048]{1,0:T(8,128)(2,1)} %bitcast.11, s32[1024]{0:T(1024)S(1)} %broadcast_clamp_fusion), kind=kCustom, calls=%fused_computation.1 | custom fusion | bytes 8392704 | tf_op jit(solution)/shard_map/gather | solution.py:43
  655.9 3.4 fusion.8
  659.3 1.1 copy.19
  (20 shorter events, 0.1 us)
Async XLA Ops:
  6.5 15.8 %copy-start = (bf16[128,4096]{1,0:T(8,128)(2,1)S(1)}, bf16[128,4096]{1,0:T(8,128)(2,1)}, u32[]{:S(2)}) copy-start(bf16[128,4096]{1,0:T(8,128)(2,1)} %param.6) | copy-start | bytes 3145732
  6.5 493.0 %reduce-scatter.2.cloned.1.call-start = ((), (), s32[]{:S(2)}) async-start(), calls=%async_computation.3 | async-start | bytes 18874368 | tf_op jit(solution)/shard_map/reduce_scatter | solution.py:34
  38.2 278.6 %copy-start.3 = (bf16[1,4096,768]{2,1,0:T(8,128)(2,1)S(1)}, bf16[1,4096,768]{2,1,0:T(8,128)(2,1)}, u32[]{:S(2)}) copy-start(bf16[1,4096,768]{2,1,0:T(8,128)(2,1)} %param.10) | copy-start | bytes 18874372
  316.8 25.0 %slice-start = ((s8[6291456]{0:T(1024)(128)(4,1)}), s8[2097152]{0:T(1024)(128)(4,1)S(1)}, s32[]{:S(2)}) async-start(s8[6291456]{0:T(1024)(128)(4,1)} %bitcast.59), calls=%async_computation.4 | async-start | bytes 4194304
  328.3 13.5 %slice-start.1 = ((s8[6291456]{0:T(1024)(128)(4,1)}), s8[4194304]{0:T(1024)(128)(4,1)S(1)}, s32[]{:S(2)}) async-start(s8[6291456]{0:T(1024)(128)(4,1)} %bitcast.59), calls=%async_computation.5 | async-start | bytes 8388608
  499.5 6.5 copy-start.2
  499.5 143.9 %all-to-all-start.1 = ((bf16[16,96,2048]{2,1,0:T(8,128)(2,1)}), bf16[16,96,2048]{2,1,0:T(8,128)(2,1)}, u32[]{:S(2)}, u32[]{:S(2)}) async-start(bf16[16,96,2048]{2,1,0:T(8,128)(2,1)} %bitcast.51), calls=%async_computation.2 | async-start | bytes 12582912 | tf_op jit(solution)/shard_map/all_to_all | solution.py:40
  643.4 17.0 %copy-start.1 = (bf16[128,4096]{1,0:T(8,128)(2,1)S(1)}, bf16[128,4096]{1,0:T(8,128)(2,1)}, u32[]{:S(2)}) copy-start(bf16[128,4096]{1,0:T(8,128)(2,1)} %param.6) | copy-start | bytes 3145732
Sparse Core Ops, SparseCore 0:
  354.3 145.1 reduce-scatter.1
where the time goes:
time: 668 us; the launch traced here: 667 us
  waiting for transfers between devices  283 us (42%)
  blocking collectives  279 us (42%)
  matrix products  40.7 us (6%)
  local copies, waits for them, and re-layouts  33.6 us (5%)
  between operations  13.5 us (2%)
  other arithmetic  11.7 us (2%)
    all_to_all x1, blocking collectives, shards(): lax.all_to_all(outgoing, 'expert', split_axis=0, concat_axis=0, tiled=True)  279 us
    reduce_scatter x1, waiting for transfers between devices, shards(): lax.psum_scatter(partial_value.astype(jnp.bfloat16), 'tensor', scatter_di...  145 us
    all_to_all x1, waiting for transfers between devices, shards(): lax.all_to_all(going_back, 'expert', split_axis=0, concat_axis=0, tiled=T...  137 us
    dot_general x1, matrix products, shards(): jnp.einsum('erd,edf->erf', rows, gate_w, preferred_element_type=jnp.float32)  13.5 us
  transfers between devices with their start and end apart: 2, of which 2 were waited for; matrix products, arithmetic and copies ran while one was open for 0% of the time, Pallas kernels for 0%

commit v1 on v0

v1 whole, which is shorter than its diff:
```python
import jax
import jax.numpy as jnp
from jax import lax
from jax.sharding import PartitionSpec as P


def shards(tokens, expert_ids, route_weights, gate_w, up_w, down_w):
    local_experts = gate_w.shape[0]
    experts_all = local_experts * lax.axis_size("expert")
    chosen = expert_ids[:, :, None] == jnp.arange(experts_all, dtype=jnp.int32)
    table = jnp.sum(jnp.where(chosen, route_weights[:, :, None], 0.0), axis=1)
    table_all = lax.all_gather(table, "expert", axis=0, tiled=True)
    tokens_all = lax.all_gather(tokens, "expert", axis=0, tiled=True)
    first = lax.axis_index("expert") * local_experts
    total = None
    for e in range(local_experts):
        mine = lax.dynamic_slice_in_dim(table_all, first + e, 1, axis=1)
        gate = jnp.dot(tokens_all, gate_w[e], preferred_element_type=jnp.float32)
        up_part = jnp.dot(tokens_all, up_w[e], preferred_element_type=jnp.float32)
        hidden = (jax.nn.silu(gate) * up_part * mine).astype(jnp.bfloat16)
        part = jnp.dot(hidden, down_w[e], preferred_element_type=jnp.float32)
        total = part if total is None else total + part
    total = total.astype(jnp.bfloat16)
    total = lax.psum_scatter(total, "expert", scatter_dimension=0, tiled=True)
    return lax.psum_scatter(total, "tensor", scatter_dimension=1, tiled=True)


def solution(mesh):
    in_specs = (
        P(("groups", "expert"), None),
        P(("groups", "expert"), None),
        P(("groups", "expert"), None),
        P("expert", None, "tensor"),
        P("expert", None, "tensor"),
        P("expert", "tensor", None),
    )
    out_specs = P(("groups", "expert"), "tensor")
    return jax.shard_map(shards, mesh=mesh, in_specs=in_specs, out_specs=out_specs, check_vma=False)
```

time: 668 us -> 400 us (0.60)
  the two profiles are of different devices: /device:TPU:13 before, /device:TPU:0 now
where the time goes in v1:
time: 400 us
  waiting for transfers between devices  307 us (77%)
  matrix products  55.4 us (14%)
  blocking collectives  23.9 us (6%)
  between operations  13.1 us (3%)
    reduce_scatter x1, waiting for transfers between devices, shards(): total = lax.psum_scatter(total, 'expert', scatter_dimension=0, tiled=True)  177 us
    all_gather x1, waiting for transfers between devices, shards(): tokens_all = lax.all_gather(tokens, 'expert', axis=0, tiled=True)  108 us
    all_gather x1, blocking collectives, shards(): table_all = lax.all_gather(table, 'expert', axis=0, tiled=True)  23.9 us
    reduce_scatter x1, waiting for transfers between devices, shards(): return lax.psum_scatter(total, 'tensor', scatter_dimension=1, tiled=True)  21.6 us
    dot_general x1, matrix products, shards(): up_part = jnp.dot(tokens_all, up_w[e], preferred_element_type=jnp.float32)  19.5 us
    dot_general x1, matrix products, shards(): gate = jnp.dot(tokens_all, gate_w[e], preferred_element_type=jnp.float32)  19.5 us
    dot_general x1, matrix products, shards(): part = jnp.dot(hidden, down_w[e], preferred_element_type=jnp.float32)  16.4 us
  transfers between devices with their start and end apart: 3, of which 3 were waited for; matrix products, arithmetic and copies ran while one was open for 0% of the time, Pallas kernels for 0%

profile of v1, /device:TPU:0, one launch (start us, length us, event | category | flops | bytes accessed | tf_op | source)
XLA Modules:
  0.0 400.2 jit_solution(8247206261162302404)
XLA Ops:
  6.5 0.0 all-gather.2.cloned.1.call-start
  6.5 0.7 all-gather.2.cloned.1.call-update
  7.3 0.0 reduce-scatter.3.cloned.1.call-start
  7.3 0.7 select_reduce_fusion
  8.0 23.9 %all_gather.7 = f32[2048,16]{0,1:T(8,128)S(1)} all-gather(f32[128,16]{0,1:T(8,128)S(1)} %select_reduce_fusion), channel_id=1, replica_groups=mesh['groups'=1,'expert'=16,'tensor'=2] {'expert'}, dimensions={0}, use_global_device_ids=true | all-gather | bytes 139264 | tf_op jit(solution)/shard_map/all_gather | solution.py:12
  31.9 107.8 %all-gather.2.cloned.1.call-done = bf16[2048,4096]{1,0:T(8,128)(2,1)} async-done(((bf16[128,4096]{1,0:T(8,128)(2,1)}), bf16[2048,4096]{1,0:T(8,128)(2,1)}) %all-gather.2.cloned.1.call-update) | async-done | bytes 16777232 | tf_op jit(solution)/shard_map/all_gather | solution.py:13
  139.7 0.0 slice-start
  139.7 19.5 %fusion.1 = f32[2048,768]{1,0:T(8,128)} fusion(bf16[2048,4096]{1,0:T(8,128)(2,1)} %all-gather.2.cloned.1.call-done, bf16[1,4096,768]{2,1,0:T(8,128)(2,1)} %param.10), kind=kOutput, calls=%fused_computation.2 | convolution fusion | flops 12884901888 | bytes 29360128 | tf_op jit(solution)/shard_map/dot_general | solution.py:19
  159.2 0.0 slice-start.1
  159.2 19.5 %multiply_convert_fusion = bf16[2048,768]{1,0:T(8,128)(2,1)S(1)} fusion(f32[2048,768]{1,0:T(8,128)} %fusion.1, bf16[2048,4096]{1,0:T(8,128)(2,1)} %all-gather.2.cloned.1.call-done, bf16[1,4096,768]{2,1,0:T(8,128)(2,1)} %param.9, f32[2048]{0:T(1024)S(1)} %bitcast.15), kind=kOutput, calls=%fused_computation.6 | convolution fusion | flops 12895911936 | bytes 32514048 | tf_op jit(solution)/shard_map/dot_general | solution.py:18
  178.7 0.0 slice-done
  178.7 0.0 slice-done.1
  178.7 16.4 %convolution_convert_fusion = bf16[2048,4096]{1,0:T(8,128)(2,1)} fusion(bf16[2048,768]{1,0:T(8,128)(2,1)S(1)} %multiply_convert_fusion, bf16[1,768,4096]{2,1,0:T(8,128)(2,1)S(1)} %bitcast.17), kind=kOutput, calls=%fused_computation | convolution fusion | flops 12893290496 | bytes 26214400 | tf_op jit(solution)/shard_map/dot_general | solution.py:21
  195.1 0.0 reduce-scatter.3.cloned.1.call-update
  195.1 0.0 reduce-scatter.5.cloned.1.call-start
  195.1 176.9 %reduce-scatter.3.cloned.1.call-done = bf16[128,4096]{1,0:T(8,128)(2,1)} async-done(((bf16[2048,4096]{1,0:T(8,128)(2,1)}), bf16[128,4096]{1,0:T(8,128)(2,1)}) %reduce-scatter.3.cloned.1.call-update) | async-done | bytes 1048592 | tf_op jit(solution)/shard_map/reduce_scatter | solution.py:24
  372.0 0.0 reduce-scatter.5.cloned.1.call-update
  372.1 21.6 %reduce-scatter.5.cloned.1.call-done = bf16[128,2048]{1,0:T(8,128)(2,1)} async-done(((bf16[128,4096]{1,0:T(8,128)(2,1)}), bf16[128,2048]{1,0:T(8,128)(2,1)}) %reduce-scatter.5.cloned.1.call-update) | async-done | bytes 524304 | tf_op jit(solution)/shard_map/reduce_scatter | solution.py:25
  (2 shorter events, 0.0 us)
Async XLA Ops:
  6.5 133.1 %all-gather.2.cloned.1.call-start = ((), (), s32[]{:S(2)}) async-start(), calls=%async_computation.2 | async-start | bytes 17825792 | tf_op jit(solution)/shard_map/all_gather | solution.py:13
  7.3 364.8 %reduce-scatter.3.cloned.1.call-start = ((), (), s32[]{:S(2)}) async-start(), calls=%async_computation.3 | async-start | bytes 17825792 | tf_op jit(solution)/shard_map/reduce_scatter | solution.py:24
  139.7 39.0 %slice-start = ((s8[6291456]{0:T(1024)(128)(4,1)}), s8[4194304]{0:T(1024)(128)(4,1)S(1)}, s32[]{:S(2)}) async-start(s8[6291456]{0:T(1024)(128)(4,1)} %bitcast.16), calls=%async_computation.5 | async-start | bytes 8388608
  159.2 19.5 %slice-start.1 = ((s8[6291456]{0:T(1024)(128)(4,1)}), s8[2097152]{0:T(1024)(128)(4,1)S(1)}, s32[]{:S(2)}) async-start(s8[6291456]{0:T(1024)(128)(4,1)} %bitcast.16), calls=%async_computation.6 | async-start | bytes 4194304
  195.1 198.5 %reduce-scatter.5.cloned.1.call-start = ((), (), s32[]{:S(2)}) async-start(), calls=%async_computation.4 | async-start | bytes 1572864 | tf_op jit(solution)/shard_map/reduce_scatter | solution.py:25
Sparse Core Ops, SparseCore 0:
  9.5 130.1 all-gather.1
  195.2 176.7 reduce-scatter.2
  374.3 19.2 reduce-scatter.4

commit v2 on v1

v2 whole, which is shorter than its diff:
```python
import jax
import jax.numpy as jnp
from jax import lax
from jax.sharding import PartitionSpec as P

CHUNKS = 4


def add(a, b):
    return (a.astype(jnp.float32) + b.astype(jnp.float32)).astype(jnp.bfloat16)


def line_reduce(slots, move):
    n = len(slots)
    slots = list(slots)
    if n == 1:
        return slots[0]
    if n == 2:
        return add(slots[0], move(slots[1], [(0, 1), (1, 0)]))
    for s in range(n - 1):
        right = move(slots[s + 1], [(i, i + 1) for i in range(s + 1)])
        left = move(slots[n - 1 - s], [(i, i - 1) for i in range(n - 1 - s, n)])
        slots[(s + 2) % n] = add(slots[(s + 2) % n], right)
        slots[n - 2 - s] = add(slots[n - 2 - s], left)
    return slots[0]


def make(mesh):
    experts, nx = mesh.shape["expert"], mesh.shape["tensor"]
    nc = 2 if experts % 2 == 0 else 1
    ny = 2 if experts // nc == 8 else 1
    nz = experts // (nc * ny)

    def index(z, y, c):
        return (z * ny + y) * nc + c

    def move_z(a, pairs):
        return lax.ppermute(a, "expert", [
            (index(s, y, c), index(t, y, c)) for s, t in pairs for y in range(ny) for c in range(nc)])

    def move_y(a, pairs):
        return lax.ppermute(a, "expert", [
            (index(z, s, c), index(z, t, c)) for s, t in pairs for z in range(nz) for c in range(nc)])

    def move_c(a, pairs):
        return lax.ppermute(a, "expert", [
            (index(z, y, s), index(z, y, t)) for s, t in pairs for z in range(nz) for y in range(ny)])

    def move_x(a, pairs):
        return lax.ppermute(a, "tensor", pairs)

    def shards(tokens, expert_ids, route_weights, gate_w, up_w, down_w):
        rows, width = tokens.shape
        local_experts = gate_w.shape[0]
        experts_all = local_experts * experts
        me = lax.axis_index("expert")
        z, y, c = me // (ny * nc), (me // nc) % ny, me % nc
        x = lax.axis_index("tensor")
        chosen = expert_ids[:, :, None] == jnp.arange(experts_all, dtype=jnp.int32)
        table = jnp.sum(jnp.where(chosen, route_weights[:, :, None], 0.0), axis=1)
        table_all = lax.all_gather(table, "expert", axis=0, tiled=True)
        tokens_all = lax.all_gather(tokens, "expert", axis=0, tiled=True)
        hidden = []
        for e in range(local_experts):
            mine = lax.dynamic_slice_in_dim(table_all, me * local_experts + e, 1, axis=1)
            gate = jnp.dot(tokens_all, gate_w[e], preferred_element_type=jnp.float32)
            up_part = jnp.dot(tokens_all, up_w[e], preferred_element_type=jnp.float32)
            hidden.append((jax.nn.silu(gate) * up_part * mine).astype(jnp.bfloat16))
        hidden = jnp.concatenate(hidden, axis=1) if local_experts > 1 else hidden[0]
        down = down_w.reshape(-1, width)
        depth = down.shape[0]
        order = [index((z - jz) % nz, (y - jy) % ny, (c - jc) % nc)
                 for jc in range(nc) for jy in range(ny) for jz in range(nz)]
        blocks = hidden.reshape(experts, rows, depth)
        blocks = jnp.take(blocks, jnp.stack(order), axis=0)
        blocks = blocks.reshape(nc, ny, nz * rows, depth)
        share = width // nx
        downs = [lax.dynamic_slice_in_dim(down, ((x - jx) % nx) * share, share, axis=1) for jx in range(nx)]
        part = share // CHUNKS

        def product(jc, jy, jx, k):
            return jnp.dot(blocks[jc, jy], downs[jx][:, k * part:(k + 1) * part],
                           preferred_element_type=jnp.float32)

        out = []
        for k in range(CHUNKS):
            held = {}
            for jy in reversed(range(ny)):
                for jx in reversed(range(nx)):
                    value = product(0, jy, jx, k)
                    if nc == 2:
                        other = move_c(product(1, jy, jx, k).astype(jnp.bfloat16), [(0, 1), (1, 0)])
                        value = value + other.astype(jnp.float32)
                    held[jy, jx] = value.astype(jnp.bfloat16)
            if k % 2 == 0:
                ys = [line_reduce([held[jy, jx] for jx in range(nx)], move_x) for jy in reversed(range(ny))][::-1]
                mine = line_reduce(ys, move_y)
            else:
                xs = [line_reduce([held[jy, jx] for jy in range(ny)], move_y) for jx in reversed(range(nx))][::-1]
                mine = line_reduce(xs, move_x)
            mine = mine.reshape(nz, rows, part)
            out.append(line_reduce([mine[jz] for jz in range(nz)], move_z))
        return jnp.concatenate(out, axis=1)

    return shards


def solution(mesh):
    in_specs = (
        P(("groups", "expert"), None),
        P(("groups", "expert"), None),
        P(("groups", "expert"), None),
        P("expert", None, "tensor"),
        P("expert", None, "tensor"),
        P("expert", "tensor", None),
    )
    out_specs = P(("groups", "expert"), "tensor")
    return jax.shard_map(make(mesh), mesh=mesh, in_specs=in_specs, out_specs=out_specs, check_vma=False)
```

time: 400 us -> 349 us (0.87)
  waiting for transfers between devices: 307 us -> 169 us
  starting transfers between devices: 0.08 us -> 66.4 us
  local copies, waits for them, and re-layouts: 0.02 us -> 12 us
    reduce_scatter x2 -> x0, waiting for transfers between devices: 198 us -> none  [the longest x1 177 us: shards(): total = lax.psum_scatter(total, 'expert', scatter_dimension=0, tiled=True)]
    ppermute x0 -> x52, waiting for transfers between devices: none -> 68.1 us  [the longest x6 44.3 us: move_x(): return lax.ppermute(a, 'tensor', pairs)]
    ppermute x0 -> x52, starting transfers between devices: none -> 66.4 us  [the longest x24 53.4 us: move_z(): lax.ppermute(a, 'expert', [(index(s, y, c), index(t, y, c)) for s, t in p...]
    all_gather x1, waiting for transfers between devices: 108 us -> 100 us  [shards(): tokens_all = lax.all_gather(tokens, 'expert', axis=0, tiled=True)]
    dynamic_slice x1 -> x2, local copies, waits for them, and re-layouts: 0.01 us -> 6.71 us  [the longest x1 6.7 us: shards(): lax.dynamic_slice_in_dim(down, (x - jx) % nx * share, share, axis=1)]
    dot_general x1 -> x32, matrix products: 16.4 us -> 20 us  [product(): jnp.dot(blocks[jc, jy], downs[jx][:, k * part:(k + 1) * part], preferred_...]
  transfers between devices with their start and end apart: 3 -> 53, of which waited for: 3 -> 16; matrix products, arithmetic and copies ran while one was open for 0% -> 5% of each run, Pallas kernels for 0% -> 0%
where the time goes in v2:
time: 349 us; the launch traced here: 348 us
  waiting for transfers between devices  169 us (48%)
  starting transfers between devices  66.4 us (19%)
  matrix products  58 us (17%)
  blocking collectives  23.9 us (7%)
  between operations  14.6 us (4%)
  local copies, waits for them, and re-layouts  12 us (3%)
  other arithmetic  4.29 us (1%)
    all_gather x1, waiting for transfers between devices, shards(): tokens_all = lax.all_gather(tokens, 'expert', axis=0, tiled=True)  100 us
    ppermute x24, starting transfers between devices, move_z(): lax.ppermute(a, 'expert', [(index(s, y, c), index(t, y, c)) for s, t in p...  53.4 us
    ppermute x6, waiting for transfers between devices, move_x(): return lax.ppermute(a, 'tensor', pairs)  44.3 us
    all_gather x1, blocking collectives, shards(): table_all = lax.all_gather(table, 'expert', axis=0, tiled=True)  23.9 us
    dot_general x32, matrix products, product(): jnp.dot(blocks[jc, jy], downs[jx][:, k * part:(k + 1) * part], preferred_...  20 us
    dot_general x1, matrix products, shards(): gate = jnp.dot(tokens_all, gate_w[e], preferred_element_type=jnp.float32)  19.8 us
    dot_general x1, matrix products, shards(): up_part = jnp.dot(tokens_all, up_w[e], preferred_element_type=jnp.float32)  18.2 us
    ppermute x6, waiting for transfers between devices, move_y(): lax.ppermute(a, 'expert', [(index(z, s, c), index(z, t, c)) for s, t in p...  17.6 us
  transfers between devices with their start and end apart: 53, of which 16 were waited for; matrix products, arithmetic and copies ran while one was open for 5% of the time, Pallas kernels for 0%

profile of v2, /device:TPU:0, one launch (start us, length us, event | category | flops | bytes accessed | tf_op | source)
XLA Modules:
  0.0 348.2 jit_solution(3679292760049061698)
XLA Ops:
  8.6 23.9 %all_gather.7 = f32[2048,16]{0,1:T(8,128)S(1)} all-gather(f32[128,16]{0,1:T(8,128)S(1)} %select_reduce_fusion), channel_id=1, replica_groups=mesh['groups'=1,'expert'=16,'tensor'=2] {'expert'}, dimensions={0}, use_global_device_ids=true | all-gather | bytes 139264 | tf_op jit(solution)/shard_map/all_gather | solution.py:61
  32.5 6.7 %dynamic-slice_bitcast_fusion.1 = (bf16[768,2048]{1,0:T(8,128)(2,1)}, bf16[768,2048]{1,0:T(8,128)(2,1)}) fusion(bf16[1,768,4096]{2,1,0:T(8,128)(2,1)} %param.11, s32[]{:T(128)S(6)} %select_n.191, s32[]{:T(128)S(6)} %select_n.193), kind=kLoop, calls=%fused_computation.7 | loop fusion | bytes 12582920 | tf_op jit(solution)/shard_map/dynamic_slice | solution.py:78
  39.2 100.1 %all-gather.2.cloned.1.call-done = bf16[2048,4096]{1,0:T(8,128)(2,1)} async-done(((bf16[128,4096]{1,0:T(8,128)(2,1)}), bf16[2048,4096]{1,0:T(8,128)(2,1)}) %all-gather.2.cloned.1.call-update) | async-done | bytes 16777232 | tf_op jit(solution)/shard_map/all_gather | solution.py:62
  139.3 18.2 %fusion = f32[2048,768]{1,0:T(8,128)S(1)} fusion(bf16[2048,4096]{1,0:T(8,128)(2,1)} %all-gather.2.cloned.1.call-done, bf16[1,4096,768]{2,1,0:T(8,128)(2,1)} %param.10), kind=kOutput, calls=%fused_computation.1 | convolution fusion | flops 12884901888 | bytes 29360128 | tf_op jit(solution)/shard_map/dot_general | solution.py:67
  157.5 19.8 %multiply_convert_fusion = bf16[2048,768]{1,0:T(8,128)(2,1)} fusion(f32[2048,768]{1,0:T(8,128)S(1)} %fusion, bf16[2048,4096]{1,0:T(8,128)(2,1)} %all-gather.2.cloned.1.call-done, bf16[1,4096,768]{2,1,0:T(8,128)(2,1)} %param.9, f32[2048]{0:T(1024)S(1)} %bitcast.93), kind=kOutput, calls=%fused_computation.5 | convolution fusion | flops 12895911936 | bytes 32514048 | tf_op jit(solution)/shard_map/dot_general | solution.py:66
  177.3 2.6 gather_fusion
  204.8 1.5 collective-permute-start.5
  208.2 10.7 %collective-permute-done.5 = bf16[512,512]{0,1:T(8,128)(2,1)S(1)} collective-permute-done((bf16[512,512]{0,1:T(8,128)(2,1)S(1)}, bf16[512,512]{0,1:T(8,128)(2,1)S(1)}, u32[]{:S(2)}, u32[]{:S(2)}) %collective-permute-start.5) | collective-permute-done | bytes 524320 | tf_op jit(solution)/shard_map/ppermute | solution.py:50
  218.9 1.5 collective-permute-start.31
  222.2 11.5 %collective-permute-done.31 = bf16[512,512]{0,1:T(8,128)(2,1)S(1)} collective-permute-done((bf16[512,512]{0,1:T(8,128)(2,1)S(1)}, bf16[512,512]{0,1:T(8,128)(2,1)S(1)}, u32[]{:S(2)}, u32[]{:S(2)}) %collective-permute-start.31) | collective-permute-done | bytes 524320 | tf_op jit(solution)/shard_map/ppermute | solution.py:50
  236.4 7.0 %collective-permute-done.2 = bf16[512,512]{0,1:T(8,128)(2,1)S(1)} collective-permute-done((bf16[512,512]{0,1:T(8,128)(2,1)S(1)}, bf16[512,512]{0,1:T(8,128)(2,1)S(1)}, u32[]{:S(2)}, u32[]{:S(2)}) %collective-permute-start.2) | collective-permute-done | bytes 524320 | tf_op jit(solution)/shard_map/ppermute | solution.py:50
  243.9 4.0 %collective-permute-done.6 = bf16[512,512]{0,1:T(8,128)(2,1)S(1)} collective-permute-done((bf16[512,512]{0,1:T(8,128)(2,1)S(1)}, bf16[512,512]{0,1:T(8,128)(2,1)S(1)}, u32[]{:S(2)}, u32[]{:S(2)}) %collective-permute-start.6) | collective-permute-done | bytes 524320 | tf_op jit(solution)/shard_map/ppermute | solution.py:42
  248.2 2.1 collective-permute-start.28
  250.3 7.1 %collective-permute-done.15 = bf16[512,512]{0,1:T(8,128)(2,1)S(1)} collective-permute-done((bf16[512,512]{0,1:T(8,128)(2,1)S(1)}, bf16[512,512]{0,1:T(8,128)(2,1)S(1)}, u32[]{:S(2)}, u32[]{:S(2)}) %collective-permute-start.15) | collective-permute-done | bytes 524320 | tf_op jit(solution)/shard_map/ppermute | solution.py:42
  258.0 4.7 %collective-permute-done.19 = bf16[512,512]{0,1:T(8,128)(2,1)S(1)} collective-permute-done((bf16[512,512]{0,1:T(8,128)(2,1)S(1)}, bf16[512,512]{0,1:T(8,128)(2,1)S(1)}, u32[]{:S(2)}, u32[]{:S(2)}) %collective-permute-start.19) | collective-permute-done | bytes 524320 | tf_op jit(solution)/shard_map/ppermute | solution.py:50
  263.7 10.3 %collective-permute-done.28 = bf16[512,512]{0,1:T(8,128)(2,1)S(1)} collective-permute-done((bf16[512,512]{0,1:T(8,128)(2,1)S(1)}, bf16[512,512]{0,1:T(8,128)(2,1)S(1)}, u32[]{:S(2)}, u32[]{:S(2)}) %collective-permute-start.28) | collective-permute-done | bytes 524320 | tf_op jit(solution)/shard_map/ppermute | solution.py:50
  274.0 1.5 collective-permute-start.7
  275.5 5.5 %collective-permute-done.32 = bf16[512,512]{0,1:T(8,128)(2,1)S(1)} collective-permute-done((bf16[512,512]{0,1:T(8,128)(2,1)S(1)}, bf16[512,512]{0,1:T(8,128)(2,1)S(1)}, u32[]{:S(2)}, u32[]{:S(2)}) %collective-permute-start.32) | collective-permute-done | bytes 524320 | tf_op jit(solution)/shard_map/ppermute | solution.py:42
  282.0 1.6 collective-permute-start.20
  284.2 1.3 collective-permute-start.33
  286.6 1.3 collective-permute-start.46
  289.4 3.8 %collective-permute-start.9 = (bf16[128,512]{0,1:T(8,128)(2,1)S(1)}, bf16[128,512]{0,1:T(8,128)(2,1)S(1)}, u32[]{:S(2)}, u32[]{:S(2)}) collective-permute-start(bf16[128,512]{0,1:T(8,128)(2,1)S(1)} %add_convert_fusion.50), channel_id=1, source_target_pairs={{0,8},{2,10},{4,12},{6,14},{8,16},{10,18},{12,20},{14,22},{1,9},{3... | collective-permute-start | bytes 393224 | tf_op jit(solution)/shard_map/ppermute | solution.py:38
  293.2 6.3 %collective-permute-start.22 = (bf16[128,512]{0,1:T(8,128)(2,1)S(1)}, bf16[128,512]{0,1:T(8,128)(2,1)S(1)}, u32[]{:S(2)}, u32[]{:S(2)}) collective-permute-start(bf16[128,512]{0,1:T(8,128)(2,1)S(1)} %add_convert_fusion.44), channel_id=1, source_target_pairs={{0,8},{2,10},{4,12},{6,14},{8,16},{10,18},{12,20},{14,22},{1,9},{3... | collective-permute-start | bytes 393224 | tf_op jit(solution)/shard_map/ppermute | solution.py:38
  300.3 2.5 collective-permute-start.35
  303.6 5.2 %collective-permute-start.48 = (bf16[128,512]{0,1:T(8,128)(2,1)S(1)}, bf16[128,512]{0,1:T(8,128)(2,1)S(1)}, u32[]{:S(2)}, u32[]{:S(2)}) collective-permute-start(bf16[128,512]{0,1:T(8,128)(2,1)S(1)} %add_convert_fusion.32), channel_id=1, source_target_pairs={{0,8},{2,10},{4,12},{6,14},{8,16},{10,18},{12,20},{14,22},{1,9},{3... | collective-permute-start | bytes 393224 | tf_op jit(solution)/shard_map/ppermute | solution.py:38
  309.5 5.2 %collective-permute-start.10 = (bf16[128,512]{0,1:T(8,128)(2,1)S(1)}, bf16[128,512]{0,1:T(8,128)(2,1)S(1)}, u32[]{:S(2)}, u32[]{:S(2)}) collective-permute-start(bf16[128,512]{0,1:T(8,128)(2,1)S(1)} %get-tuple-element.7), channel_id=1, source_target_pairs={{0,8},{2,10},{4,12},{6,14},{8,16},{10,18},{12,20},{14,22},{16,24},... | collective-permute-start | bytes 393224 | tf_op jit(solution)/shard_map/ppermute | solution.py:38
  314.8 1.3 collective-permute-start.12
  316.1 5.2 %collective-permute-start.23 = (bf16[128,512]{0,1:T(8,128)(2,1)S(1)}, bf16[128,512]{0,1:T(8,128)(2,1)S(1)}, u32[]{:S(2)}, u32[]{:S(2)}) collective-permute-start(bf16[128,512]{0,1:T(8,128)(2,1)S(1)} %get-tuple-element.11), channel_id=1, source_target_pairs={{0,8},{2,10},{4,12},{6,14},{8,16},{10,18},{12,20},{14,22},{16,24},... | collective-permute-start | bytes 393224 | tf_op jit(solution)/shard_map/ppermute | solution.py:38
  321.4 1.3 collective-permute-start.25
  322.7 4.6 %collective-permute-start.36 = (bf16[128,512]{0,1:T(8,128)(2,1)S(1)}, bf16[128,512]{0,1:T(8,128)(2,1)S(1)}, u32[]{:S(2)}, u32[]{:S(2)}) collective-permute-start(bf16[128,512]{0,1:T(8,128)(2,1)S(1)} %get-tuple-element.15), channel_id=1, source_target_pairs={{0,8},{2,10},{4,12},{6,14},{8,16},{10,18},{12,20},{14,22},{16,24},... | collective-permute-start | bytes 393224 | tf_op jit(solution)/shard_map/ppermute | solution.py:38
  328.7 4.6 %collective-permute-start.49 = (bf16[128,512]{0,1:T(8,128)(2,1)S(1)}, bf16[128,512]{0,1:T(8,128)(2,1)S(1)}, u32[]{:S(2)}, u32[]{:S(2)}) collective-permute-start(bf16[128,512]{0,1:T(8,128)(2,1)S(1)} %get-tuple-element.19), channel_id=1, source_target_pairs={{0,8},{2,10},{4,12},{6,14},{8,16},{10,18},{12,20},{14,22},{16,24},... | collective-permute-start | bytes 393224 | tf_op jit(solution)/shard_map/ppermute | solution.py:38
  335.8 4.4 %collective-permute-done.51 = bf16[128,512]{0,1:T(8,128)(2,1)S(1)} collective-permute-done((bf16[128,512]{0,1:T(8,128)(2,1)S(1)}, bf16[128,512]{0,1:T(8,128)(2,1)S(1)}, u32[]{:S(2)}, u32[]{:S(2)}) %collective-permute-start.51) | collective-permute-done | bytes 131104 | tf_op jit(solution)/shard_map/ppermute | solution.py:38
  (153 shorter events, 46.5 us)
Async XLA Ops:
  6.5 132.8 %all-gather.2.cloned.1.call-start = ((), (), s32[]{:S(2)}) async-start(), calls=%async_computation | async-start | bytes 17825792 | tf_op jit(solution)/shard_map/all_gather | solution.py:62
  196.5 39.3 %collective-permute-start = (bf16[512,512]{0,1:T(8,128)(2,1)S(1)}, bf16[512,512]{0,1:T(8,128)(2,1)S(1)}, u32[]{:S(2)}, u32[]{:S(2)}) collective-permute-start(bf16[512,512]{0,1:T(8,128)(2,1)S(1)} %convolution_convert_fusion.15), channel_id=1, source_target_pairs={{0,2},{4,6},{8,10},{12,14},{16,18},{20,22},{24,26},{28,30},{2,0},{... | collective-permute-start | bytes 1572872 | tf_op jit(solution)/shard_map/ppermute | solution.py:46
  199.4 21.1 %collective-permute-start.16 = (bf16[512,512]{0,1:T(8,128)(2,1)S(1)}, bf16[512,512]{0,1:T(8,128)(2,1)S(1)}, u32[]{:S(2)}, u32[]{:S(2)}) collective-permute-start(bf16[512,512]{0,1:T(8,128)(2,1)S(1)} %convolution_convert_fusion.9), channel_id=1, source_target_pairs={{0,2},{4,6},{8,10},{12,14},{16,18},{20,22},{24,26},{28,30},{2,0},{... | collective-permute-start | bytes 1572872 | tf_op jit(solution)/shard_map/ppermute | solution.py:46
  204.8 14.1 %collective-permute-start.5 = (bf16[512,512]{0,1:T(8,128)(2,1)S(1)}, bf16[512,512]{0,1:T(8,128)(2,1)S(1)}, u32[]{:S(2)}, u32[]{:S(2)}) collective-permute-start(bf16[512,512]{0,1:T(8,128)(2,1)S(1)} %add_convert_fusion.23), channel_id=1, source_target_pairs={{0,1},{1,0},{2,3},{3,2},{4,5},{5,4},{6,7},{7,6},{8,9},{9,8},{10,11... | collective-permute-start | bytes 1572872 | tf_op jit(solution)/shard_map/ppermute | solution.py:50
  206.9 13.9 %collective-permute-start.18 = (bf16[512,512]{0,1:T(8,128)(2,1)S(1)}, bf16[512,512]{0,1:T(8,128)(2,1)S(1)}, u32[]{:S(2)}, u32[]{:S(2)}) collective-permute-start(bf16[512,512]{0,1:T(8,128)(2,1)S(1)} %add_convert_fusion.16), channel_id=1, source_target_pairs={{0,4},{2,6},{8,12},{10,14},{16,20},{18,22},{24,28},{26,30},{4,0},{... | collective-permute-start | bytes 1572872 | tf_op jit(solution)/shard_map/ppermute | solution.py:42
  208.1 13.4 %collective-permute-start.29 = (bf16[512,512]{0,1:T(8,128)(2,1)S(1)}, bf16[512,512]{0,1:T(8,128)(2,1)S(1)}, u32[]{:S(2)}, u32[]{:S(2)}) collective-permute-start(bf16[512,512]{0,1:T(8,128)(2,1)S(1)} %convolution_convert_fusion.5), channel_id=1, source_target_pairs={{0,2},{4,6},{8,10},{12,14},{16,18},{20,22},{24,26},{28,30},{2,0},{... | collective-permute-start | bytes 1572872 | tf_op jit(solution)/shard_map/ppermute | solution.py:46
  218.9 14.9 %collective-permute-start.31 = (bf16[512,512]{0,1:T(8,128)(2,1)S(1)}, bf16[512,512]{0,1:T(8,128)(2,1)S(1)}, u32[]{:S(2)}, u32[]{:S(2)}) collective-permute-start(bf16[512,512]{0,1:T(8,128)(2,1)S(1)} %add_convert_fusion.9), channel_id=1, source_target_pairs={{0,1},{1,0},{2,3},{3,2},{4,5},{5,4},{6,7},{7,6},{8,9},{9,8},{10,11... | collective-permute-start | bytes 1572872 | tf_op jit(solution)/shard_map/ppermute | solution.py:50
  220.6 13.9 %collective-permute-start.42 = (bf16[512,512]{0,1:T(8,128)(2,1)S(1)}, bf16[512,512]{0,1:T(8,128)(2,1)S(1)}, u32[]{:S(2)}, u32[]{:S(2)}) collective-permute-start(bf16[512,512]{0,1:T(8,128)(2,1)S(1)} %convolution_convert_fusion.1), channel_id=1, source_target_pairs={{0,2},{4,6},{8,10},{12,14},{16,18},{20,22},{24,26},{28,30},{2,0},{... | collective-permute-start | bytes 1572872 | tf_op jit(solution)/shard_map/ppermute | solution.py:46
  220.8 14.8 %collective-permute-start.44 = (bf16[512,512]{0,1:T(8,128)(2,1)S(1)}, bf16[512,512]{0,1:T(8,128)(2,1)S(1)}, u32[]{:S(2)}, u32[]{:S(2)}) collective-permute-start(bf16[512,512]{0,1:T(8,128)(2,1)S(1)} %add_convert_fusion.2), channel_id=1, source_target_pairs={{0,4},{2,6},{8,12},{10,14},{16,20},{18,22},{24,28},{26,30},{4,0},{... | collective-permute-start | bytes 1572872 | tf_op jit(solution)/shard_map/ppermute | solution.py:42
  221.6 21.8 %collective-permute-start.2 = (bf16[512,512]{0,1:T(8,128)(2,1)S(1)}, bf16[512,512]{0,1:T(8,128)(2,1)S(1)}, u32[]{:S(2)}, u32[]{:S(2)}) collective-permute-start(bf16[512,512]{0,1:T(8,128)(2,1)S(1)} %add_convert_fusion.26), channel_id=1, source_target_pairs={{0,1},{1,0},{2,3},{3,2},{4,5},{5,4},{6,7},{7,6},{8,9},{9,8},{10,11... | collective-permute-start | bytes 1572872 | tf_op jit(solution)/shard_map/ppermute | solution.py:50
  233.7 14.2 %collective-permute-start.6 = (bf16[512,512]{0,1:T(8,128)(2,1)S(1)}, bf16[512,512]{0,1:T(8,128)(2,1)S(1)}, u32[]{:S(2)}, u32[]{:S(2)}) collective-permute-start(bf16[512,512]{0,1:T(8,128)(2,1)S(1)} %add_convert_fusion.22), channel_id=1, source_target_pairs={{0,4},{2,6},{8,12},{10,14},{16,20},{18,22},{24,28},{26,30},{4,0},{... | collective-permute-start | bytes 1572872 | tf_op jit(solution)/shard_map/ppermute | solution.py:42
  234.5 13.7 %collective-permute-start.13 = (bf16[512,512]{0,1:T(8,128)(2,1)S(1)}, bf16[512,512]{0,1:T(8,128)(2,1)S(1)}, u32[]{:S(2)}, u32[]{:S(2)}) collective-permute-start(bf16[512,512]{0,1:T(8,128)(2,1)S(1)} %convolution_convert_fusion.11), channel_id=1, source_target_pairs={{0,2},{4,6},{8,10},{12,14},{16,18},{20,22},{24,26},{28,30},{2,0},{... | collective-permute-start | bytes 1572872 | tf_op jit(solution)/shard_map/ppermute | solution.py:46
  235.5 28.1 %collective-permute-start.26 = (bf16[512,512]{0,1:T(8,128)(2,1)S(1)}, bf16[512,512]{0,1:T(8,128)(2,1)S(1)}, u32[]{:S(2)}, u32[]{:S(2)}) collective-permute-start(bf16[512,512]{0,1:T(8,128)(2,1)S(1)} %convolution_convert_fusion.7), channel_id=1, source_target_pairs={{0,2},{4,6},{8,10},{12,14},{16,18},{20,22},{24,26},{28,30},{2,0},{... | collective-permute-start | bytes 1572872 | tf_op jit(solution)/shard_map/ppermute | solution.py:46
  235.8 46.2 %collective-permute-start.39 = (bf16[512,512]{0,1:T(8,128)(2,1)S(1)}, bf16[512,512]{0,1:T(8,128)(2,1)S(1)}, u32[]{:S(2)}, u32[]{:S(2)}) collective-permute-start(bf16[512,512]{0,1:T(8,128)(2,1)S(1)} %convolution_convert_fusion.3), channel_id=1, source_target_pairs={{0,2},{4,6},{8,10},{12,14},{16,18},{20,22},{24,26},{28,30},{2,0},{... | collective-permute-start | bytes 1572872 | tf_op jit(solution)/shard_map/ppermute | solution.py:46
  243.4 14.1 %collective-permute-start.15 = (bf16[512,512]{0,1:T(8,128)(2,1)S(1)}, bf16[512,512]{0,1:T(8,128)(2,1)S(1)}, u32[]{:S(2)}, u32[]{:S(2)}) collective-permute-start(bf16[512,512]{0,1:T(8,128)(2,1)S(1)} %add_convert_fusion.19), channel_id=1, source_target_pairs={{0,4},{2,6},{8,12},{10,14},{16,20},{18,22},{24,28},{26,30},{4,0},{... | collective-permute-start | bytes 1572872 | tf_op jit(solution)/shard_map/ppermute | solution.py:42
  247.9 14.9 %collective-permute-start.19 = (bf16[512,512]{0,1:T(8,128)(2,1)S(1)}, bf16[512,512]{0,1:T(8,128)(2,1)S(1)}, u32[]{:S(2)}, u32[]{:S(2)}) collective-permute-start(bf16[512,512]{0,1:T(8,128)(2,1)S(1)} %add_convert_fusion.15), channel_id=1, source_target_pairs={{0,1},{1,0},{2,3},{3,2},{4,5},{5,4},{6,7},{7,6},{8,9},{9,8},{10,11... | collective-permute-start | bytes 1572872 | tf_op jit(solution)/shard_map/ppermute | solution.py:50
  248.2 25.8 %collective-permute-start.28 = (bf16[512,512]{0,1:T(8,128)(2,1)S(1)}, bf16[512,512]{0,1:T(8,128)(2,1)S(1)}, u32[]{:S(2)}, u32[]{:S(2)}) collective-permute-start(bf16[512,512]{0,1:T(8,128)(2,1)S(1)} %add_convert_fusion.12), channel_id=1, source_target_pairs={{0,1},{1,0},{2,3},{3,2},{4,5},{5,4},{6,7},{7,6},{8,9},{9,8},{10,11... | collective-permute-start | bytes 1572872 | tf_op jit(solution)/shard_map/ppermute | solution.py:50
  257.5 26.1 %collective-permute-start.41 = (bf16[512,512]{0,1:T(8,128)(2,1)S(1)}, bf16[512,512]{0,1:T(8,128)(2,1)S(1)}, u32[]{:S(2)}, u32[]{:S(2)}) collective-permute-start(bf16[512,512]{0,1:T(8,128)(2,1)S(1)} %add_convert_fusion.5), channel_id=1, source_target_pairs={{0,4},{2,6},{8,12},{10,14},{16,20},{18,22},{24,28},{26,30},{4,0},{... | collective-permute-start | bytes 1572872 | tf_op jit(solution)/shard_map/ppermute | solution.py:42
  262.8 18.2 %collective-permute-start.32 = (bf16[512,512]{0,1:T(8,128)(2,1)S(1)}, bf16[512,512]{0,1:T(8,128)(2,1)S(1)}, u32[]{:S(2)}, u32[]{:S(2)}) collective-permute-start(bf16[512,512]{0,1:T(8,128)(2,1)S(1)} %add_convert_fusion.8), channel_id=1, source_target_pairs={{0,4},{2,6},{8,12},{10,14},{16,20},{18,22},{24,28},{26,30},{4,0},{... | collective-permute-start | bytes 1572872 | tf_op jit(solution)/shard_map/ppermute | solution.py:42
  263.6 20.6 %collective-permute-start.45 = (bf16[512,512]{0,1:T(8,128)(2,1)S(1)}, bf16[512,512]{0,1:T(8,128)(2,1)S(1)}, u32[]{:S(2)}, u32[]{:S(2)}) collective-permute-start(bf16[512,512]{0,1:T(8,128)(2,1)S(1)} %add_convert_fusion.1), channel_id=1, source_target_pairs={{0,1},{1,0},{2,3},{3,2},{4,5},{5,4},{6,7},{7,6},{8,9},{9,8},{10,11... | collective-permute-start | bytes 1572872 | tf_op jit(solution)/shard_map/ppermute | solution.py:50
  286.6 13.0 %collective-permute-start.46 = (bf16[128,512]{0,1:T(8,128)(2,1)S(1)}, bf16[128,512]{0,1:T(8,128)(2,1)S(1)}, u32[]{:S(2)}, u32[]{:S(2)}) collective-permute-start(bf16[128,512]{0,1:T(8,128)(2,1)S(1)} %get-tuple-element.21), channel_id=1, source_target_pairs={{0,8},{2,10},{4,12},{6,14},{1,9},{3,11},{5,13},{7,15}} | collective-permute-start | bytes 393224 | tf_op jit(solution)/shard_map/ppermute | solution.py:38
  288.6 14.3 %collective-permute-start.11 = (bf16[128,512]{0,1:T(8,128)(2,1)S(1)}, bf16[128,512]{0,1:T(8,128)(2,1)S(1)}, u32[]{:S(2)}, u32[]{:S(2)}) collective-permute-start(bf16[128,512]{0,1:T(8,128)(2,1)S(1)} %add_convert_fusion.50), channel_id=1, source_target_pairs={{16,8},{18,10},{20,12},{22,14},{24,16},{26,18},{28,20},{30,22},{17... | collective-permute-start | bytes 393224 | tf_op jit(solution)/shard_map/ppermute | solution.py:38
  289.4 14.2 %collective-permute-start.9 = (bf16[128,512]{0,1:T(8,128)(2,1)S(1)}, bf16[128,512]{0,1:T(8,128)(2,1)S(1)}, u32[]{:S(2)}, u32[]{:S(2)}) collective-permute-start(bf16[128,512]{0,1:T(8,128)(2,1)S(1)} %add_convert_fusion.50), channel_id=1, source_target_pairs={{0,8},{2,10},{4,12},{6,14},{8,16},{10,18},{12,20},{14,22},{1,9},{3... | collective-permute-start | bytes 393224 | tf_op jit(solution)/shard_map/ppermute | solution.py:38
  293.2 15.6 %collective-permute-start.22 = (bf16[128,512]{0,1:T(8,128)(2,1)S(1)}, bf16[128,512]{0,1:T(8,128)(2,1)S(1)}, u32[]{:S(2)}, u32[]{:S(2)}) collective-permute-start(bf16[128,512]{0,1:T(8,128)(2,1)S(1)} %add_convert_fusion.44), channel_id=1, source_target_pairs={{0,8},{2,10},{4,12},{6,14},{8,16},{10,18},{12,20},{14,22},{1,9},{3... | collective-permute-start | bytes 393224 | tf_op jit(solution)/shard_map/ppermute | solution.py:38
  300.3 14.5 %collective-permute-start.35 = (bf16[128,512]{0,1:T(8,128)(2,1)S(1)}, bf16[128,512]{0,1:T(8,128)(2,1)S(1)}, u32[]{:S(2)}, u32[]{:S(2)}) collective-permute-start(bf16[128,512]{0,1:T(8,128)(2,1)S(1)} %add_convert_fusion.38), channel_id=1, source_target_pairs={{0,8},{2,10},{4,12},{6,14},{8,16},{10,18},{12,20},{14,22},{1,9},{3... | collective-permute-start | bytes 393224 | tf_op jit(solution)/shard_map/ppermute | solution.py:38
  302.9 13.2 %collective-permute-start.37 = (bf16[128,512]{0,1:T(8,128)(2,1)S(1)}, bf16[128,512]{0,1:T(8,128)(2,1)S(1)}, u32[]{:S(2)}, u32[]{:S(2)}) collective-permute-start(bf16[128,512]{0,1:T(8,128)(2,1)S(1)} %add_convert_fusion.38), channel_id=1, source_target_pairs={{16,8},{18,10},{20,12},{22,14},{24,16},{26,18},{28,20},{30,22},{17... | collective-permute-start | bytes 393224 | tf_op jit(solution)/shard_map/ppermute | solution.py:38
  303.6 17.8 %collective-permute-start.48 = (bf16[128,512]{0,1:T(8,128)(2,1)S(1)}, bf16[128,512]{0,1:T(8,128)(2,1)S(1)}, u32[]{:S(2)}, u32[]{:S(2)}) collective-permute-start(bf16[128,512]{0,1:T(8,128)(2,1)S(1)} %add_convert_fusion.32), channel_id=1, source_target_pairs={{0,8},{2,10},{4,12},{6,14},{8,16},{10,18},{12,20},{14,22},{1,9},{3... | collective-permute-start | bytes 393224 | tf_op jit(solution)/shard_map/ppermute | solution.py:38
  308.9 13.9 %collective-permute-start.50 = (bf16[128,512]{0,1:T(8,128)(2,1)S(1)}, bf16[128,512]{0,1:T(8,128)(2,1)S(1)}, u32[]{:S(2)}, u32[]{:S(2)}) collective-permute-start(bf16[128,512]{0,1:T(8,128)(2,1)S(1)} %add_convert_fusion.32), channel_id=1, source_target_pairs={{16,8},{18,10},{20,12},{22,14},{24,16},{26,18},{28,20},{30,22},{17... | collective-permute-start | bytes 393224 | tf_op jit(solution)/shard_map/ppermute | solution.py:38
  309.5 17.8 %collective-permute-start.10 = (bf16[128,512]{0,1:T(8,128)(2,1)S(1)}, bf16[128,512]{0,1:T(8,128)(2,1)S(1)}, u32[]{:S(2)}, u32[]{:S(2)}) collective-permute-start(bf16[128,512]{0,1:T(8,128)(2,1)S(1)} %get-tuple-element.7), channel_id=1, source_target_pairs={{0,8},{2,10},{4,12},{6,14},{8,16},{10,18},{12,20},{14,22},{16,24},... | collective-permute-start | bytes 393224 | tf_op jit(solution)/shard_map/ppermute | solution.py:38
  314.8 13.9 %collective-permute-start.12 = (bf16[128,512]{0,1:T(8,128)(2,1)S(1)}, bf16[128,512]{0,1:T(8,128)(2,1)S(1)}, u32[]{:S(2)}, u32[]{:S(2)}) collective-permute-start(bf16[128,512]{0,1:T(8,128)(2,1)S(1)} %get-tuple-element.8), channel_id=1, source_target_pairs={{8,0},{10,2},{12,4},{14,6},{16,8},{18,10},{20,12},{22,14},{24,16},... | collective-permute-start | bytes 393224 | tf_op jit(solution)/shard_map/ppermute | solution.py:38
  316.1 17.2 %collective-permute-start.23 = (bf16[128,512]{0,1:T(8,128)(2,1)S(1)}, bf16[128,512]{0,1:T(8,128)(2,1)S(1)}, u32[]{:S(2)}, u32[]{:S(2)}) collective-permute-start(bf16[128,512]{0,1:T(8,128)(2,1)S(1)} %get-tuple-element.11), channel_id=1, source_target_pairs={{0,8},{2,10},{4,12},{6,14},{8,16},{10,18},{12,20},{14,22},{16,24},... | collective-permute-start | bytes 393224 | tf_op jit(solution)/shard_map/ppermute | solution.py:38
  321.4 13.2 %collective-permute-start.25 = (bf16[128,512]{0,1:T(8,128)(2,1)S(1)}, bf16[128,512]{0,1:T(8,128)(2,1)S(1)}, u32[]{:S(2)}, u32[]{:S(2)}) collective-permute-start(bf16[128,512]{0,1:T(8,128)(2,1)S(1)} %get-tuple-element.12), channel_id=1, source_target_pairs={{8,0},{10,2},{12,4},{14,6},{16,8},{18,10},{20,12},{22,14},{24,16},... | collective-permute-start | bytes 393224 | tf_op jit(solution)/shard_map/ppermute | solution.py:38
  (23 other events, 135.4 us)
Sparse Core Ops, SparseCore 0:
  9.5 129.7 all-gather.1
